TPU v7x, 128 devices: a whole 4x4x4 slice. The times are simulated.
128 devices in a mesh: img: 8 (over z, y_hi), txt: 16 (over y_lo, x, core).
Axes of the slice: x: 4, y: 4 (y_hi: 2, y_lo: 2; y = y_hi * 2 + y_lo), z: 4, core: 2. Of those that a mesh axis runs over, the one named last changes fastest.
Arguments:
- img_embed: bfloat16 [16384, 1152], P(('img', 'txt')), may hold values from -0.3984375 to 0.3984375
- img_tangent: bfloat16 [16384, 1152], P(('img', 'txt')), may hold values from -0.29882812 to 0.29882812
- txt_embed: bfloat16 [16384, 1152], P(('txt', 'img')), may hold values from -0.3984375 to 0.3984375
- txt_tangent: bfloat16 [16384, 1152], P(('txt', 'img')), may hold values from -0.29882812 to 0.29882812
- labels: int32 [16384], P('img'), may hold values from 0 to 16383, each once
- log_temp: float32 [1], replicated, may hold values from 1 to 2
- bias: float32 [1], replicated, may hold values from -3 to 0
- cotangent: float32 [1], replicated, may hold values from 0.05 to 0.15
Outputs:
- grad_img: float32 [16384, 1152], P(('img', 'txt'))
- grad_img_tangent: float32 [16384, 1152], P(('img', 'txt'))
- grad_txt: float32 [16384, 1152], P(('txt', 'img'))
- grad_txt_tangent: float32 [16384, 1152], P(('txt', 'img'))
Inputs may be any that keep to these rules, and one draw needn't show every extreme that they name: `labels`: each text index is the positive of exactly one image row.
All inputs are finite; a program needn't handle non-finite values.
Results may differ from a plain program's by a relative error of at most 0.0032.
Values may be sent and summed in bfloat16 or wider, within the bound.
A program may use at most 128 MiB of HBM per device.

v0:
```python
import functools
import math

import jax
import jax.numpy as jnp
from jax import lax
from jax.experimental import pallas as pl
from jax.experimental.pallas import tpu as pltpu
from jax.sharding import PartitionSpec as P

MESH = pl.DeviceIdType.MESH
F32 = jnp.float32
BF16 = jnp.bfloat16
LOG2E = math.log2(math.e)

ORDER = (7, 4, 6, 5, 2, 3, 1, 0)
EVENTS = (
    ("t", "y6", 5), ("i", "y6", 7), ("t", "c2", 7), ("i", "c2", 8),
    ("t", "y2", 9), ("i", "y2", 10), ("t", "y3", 13), ("i", "y3", 13),
    ("t", "c1", 13), ("i", "c1", 13), ("t", "cb", 13), ("i", "cb", 13),
    ("t", "e1", 13), ("t", "ct", 14), ("i", "e1", 14), ("i", "ct", 15),
)
KEEP0 = (0, 2, 3, 6)
KEEP1 = (0, 1, 2, 5)
TILES = ((0, 0), (0, 1), (1, 0), (1, 1),
         (0, 2), (1, 2), (2, 0), (2, 1), (2, 2),
         (0, 3), (1, 3), (2, 3))


def pick(table, index):
    value = jnp.int32(table[0])
    for at, entry in enumerate(table[1:], 1):
        value = jnp.where(index == at, jnp.int32(entry), value)
    return value


def rows_at(index, size):
    return pl.ds(pl.multiple_of(index * size, size), size)


def split(D):
    return max(1, round(2 * D * 4 / 9 / 128)) * 128


class Copies:
    def __init__(self, send, recv):
        self.send, self.recv, self.table = send, recv, {}

    def add(self, name, src, dst, device):
        at = len(self.table)
        self.table[name] = pltpu.make_async_remote_copy(
            src_ref=src, dst_ref=dst, send_sem=self.send.at[at], recv_sem=self.recv.at[at],
            device_id=device, device_id_type=MESH)

    def start(self, *names):
        for name in names:
            self.table[name].start()

    def landed(self, *names):
        for name in names:
            self.table[name].wait_recv()

    def drain(self):
        for copy in self.table.values():
            copy.wait_send()


N_GATHER = 15 + 15 + 16
N_REDUCE = 17 + 17


def kernel(log_temp_in, bias_in, cotangent_in, labels_in, img_embed, img_tangent, txt_embed, txt_tangent,
           out_img, out_img_tan, out_txt, out_txt_tan,
           im, tx, tan, w, rel, rx_core, rx_i0, rx_i1, rx_t0, rx_t1, keep_i0, keep_i1, keep_t0, keep_t1,
           st_i0, st_i1, st_t0, st_t1, log_temp, bias, cotangent, labels,
           load_sem, g_send, g_recv, r_send, r_recv, c_send, c_recv):
    R, D = txt_embed.shape
    H = R // 2
    S = split(D)
    img, txt = lax.axis_index("img"), lax.axis_index("txt")
    z, y_hi = img // 2, img % 2
    y_lo, x, c = txt // 8, (txt // 2) % 4, txt % 2

    def at_txt(y_lo, x, c):
        return (y_lo * 4 + x) * 2 + c

    core = (img, at_txt(y_lo, x, 1 - c))
    i_y = (img, at_txt(1 - y_lo, x, c))
    i_p, i_m = (img, at_txt(y_lo, (x + 1) % 4, c)), (img, at_txt(y_lo, (x + 3) % 4, c))
    t_y = (z * 2 + 1 - y_hi, at_txt(1 - y_lo, x, c))
    t_p, t_m = (((z + 1) % 4) * 2 + y_hi, txt), (((z + 3) % 4) * 2 + y_hi, txt)

    loads = [
        pltpu.make_async_copy(src, dst, load_sem.at[n])
        for n, (src, dst) in enumerate((
            (img_embed, im.at[0:R, D:2 * D]), (img_tangent, im.at[0:R, 0:D]),
            (txt_embed, tx.at[0:R, 0:D]), (txt_tangent, tan),
            (log_temp_in, log_temp), (bias_in, bias), (cotangent_in, cotangent), (labels_in, labels)))
    ]
    for copy in loads:
        copy.start()
    barrier = pltpu.get_barrier_semaphore()
    peers = (core, i_y, i_p, i_m, t_y, t_p, t_m)
    for peer in peers:
        pl.semaphore_signal(barrier, inc=1, device_id=peer, device_id_type=MESH)
    for copy in loads:
        copy.wait()
    tx[0:R, D:2 * D] = (tx[0:R, 0:D].astype(F32) + tan[...].astype(F32)).astype(BF16)
    pl.semaphore_wait(barrier, len(peers))

    g = Copies(g_send, g_recv)
    families = (("i", im, 2 * R, i_y, i_p, i_m), ("t", tx, R, t_y, t_p, t_m))
    a, b = slice(S, 2 * D), slice(0, S)
    for f, buf, pitch, y, p, m in families:
        def add(name, src, dst, col, to, lo=0, hi=R, f=f, buf=buf, pitch=pitch):
            g.add(f + name, buf.at[src * pitch + lo:src * pitch + hi, col],
                  buf.at[dst * pitch + lo:dst * pitch + hi, col], to)
        add("A1", 0, 1, a, y)
        add("A3", 0, 3, a, p)
        add("A2", 0, 2, a, m)
        add("A5", 1, 5, a, p)
        add("A4", 1, 4, a, m)
        add("A6", 3, 6, a, p)
        add("A7", 4, 7, a, m)
        add("B3", 0, 3, b, p)
        add("B2", 0, 2, b, m)
        add("B6t", 3, 6, b, p, 0, H)
        add("B6b", 2, 6, b, m, H, R)
        add("B1", 0, 1, b, y)
        add("B4", 2, 4, b, y)
        add("B5", 3, 5, b, y)
        add("B7", 6, 7, b, y)
    for k in range(8):
        for name, col in (("A", a), ("B", b)):
            g.add("c%s%d" % (name, k), im.at[2 * R * k:2 * R * k + R, col],
                  im.at[2 * R * k + R:2 * R * (k + 1), col], core)

    def both(*names):
        return [f + name for name in names for f in "it"]

    g.start(*both("A1", "B3", "B2", "A3", "A2", "B1"), "cB0", "cA0")

    lane = lax.broadcasted_iota(jnp.int32, (R, R), 1)

    def place(k, _):
        shift, other = pick((0, 0, 1, 3, 1, 3, 2, 2), k // 2), pick((0, 1, 0, 0, 1, 1, 0, 1), k // 2)
        t = at_txt(jnp.where(other == 1, 1 - y_lo, y_lo), (x + shift) % 4, jnp.where(k % 2 == 1, 1 - c, c))
        row = jnp.broadcast_to(labels[pl.ds(t, 1), :], (R, R))
        rel[rows_at(k, R), :] = row.T - lane
        return 0

    lax.fori_loop(0, 16, place, 0)

    scale = jnp.exp(jnp.broadcast_to(log_temp[...], (1, R)))
    slope, shift = scale * LOG2E, jnp.broadcast_to(bias[...], (1, R)) * LOG2E
    upstream = jnp.broadcast_to(cotangent[...], (1, R))

    def add_up(lo, hi):
        def one(k, _):
            rows = rows_at(k, R)
            im[rows, 2 * D:3 * D] = (im[rows, 0:D].astype(F32) + im[rows, D:2 * D].astype(F32)).astype(BF16)
            return 0
        lax.fori_loop(2 * lo, 2 * hi, one, 0)

    def arrive(slots):
        for k in slots:
            g.landed("cA%d" % k, "cB%d" % k)

    def base_of(k):
        d, other = pick((0, 0, 1, 3, 1, 3, 2, 2), k), pick((0, 1, 0, 0, 1, 1, 0, 1), k)
        hi, lo = jnp.where(other == 1, 1 - y_hi, y_hi), jnp.where(other == 1, 1 - y_lo, y_lo)
        return (at_txt(lo, x, c) * 8 + ((z + d) % 4) * 2 + hi) * R

    def weigh(dots, rows, first, count):
        near = rel[rows, :]
        for n in range(count):
            logit = dots[:, n * R:(n + 1) * R] * slope + shift
            positive = near == base_of(first + n)
            power = jnp.exp2(jnp.where(positive, logit, -logit))
            weight = jnp.where(positive, -upstream, upstream) / (1.0 + power)
            w[rows, rows_at(first + n, R)] = weight.astype(BF16)

    def tile(s, _):
        qp, tp = pick([t[0] for t in TILES], s), pick([t[1] for t in TILES], s)
        rows, cols = rows_at(qp, 4 * R), rows_at(tp, 2 * R)
        dots = lax.dot_general(im[rows, 0:2 * D], tx[cols, :], (((1,), (1,)), ((), ())), preferred_element_type=F32)
        weigh(dots, rows, 2 * tp, 2)
        return 0

    def first():
        g.landed(*both("B3", "B2"))
        g.start(*both("B6t", "B6b", "B5", "B4"), "cB3", "cB2")
        g.landed(*both("A1"))
        g.start(*both("A5", "A4"), "cA1")
        g.landed(*both("B6t", "B6b"))
        g.start(*both("B7"), "cB6")
        g.landed(*both("A3", "A2"))
        g.start(*both("A6"), "cA3", "cA2")
        g.landed(*both("B1"))
        g.start("cB1")
        arrive((0, 1, 2, 3))
        add_up(0, 4)

    def forward():
        g.landed(*both("A4"))
        g.start(*both("A7"), "cA4")

    def second():
        for name in ("B5", "A5", "B4"):
            g.landed("i" + name)
            g.start("c" + name)
        g.landed("tB5", "tA5", "tB4")

    def second_img():
        arrive((4, 5))

    def third():
        add_up(4, 6)
        for name in ("A6", "A7", "B7"):
            g.landed("i" + name)
            g.start("c" + name)
        g.landed("tA6", "tA7", "tB7")

    def third_img():
        arrive((6, 7))

    def part(s, _):
        for at, do in ((0, first), (2, forward), (4, second), (6, second_img), (9, third)):
            @pl.when(s == at)
            def _(do=do):
                do()

        return tile(s, 0)

    lax.fori_loop(0, 12, part, 0)
    third_img()
    rows = pl.ds(12 * R, 4 * R)
    weigh(lax.dot_general(im[rows, 0:2 * D], tx[...], (((1,), (1,)), ((), ())), preferred_element_type=F32), rows, 0, 8)
    add_up(6, 8)
    g.drain()

    r = Copies(r_send, r_recv)
    reduces = (("i", rx_i0, rx_i1, keep_i0, keep_i1, st_i0, st_i1, i_y, i_p, i_m),
               ("t", rx_t0, rx_t1, keep_t0, keep_t1, st_t0, st_t1, t_y, t_p, t_m))
    left, right = ("y0", "y2", "y3", "y6", "pm", "pp", "cc"), ("c1", "f1", "g1", "c2", "f2", "g2", "e1")

    def landing(name, rx0, rx1):
        return rx0.at[left.index(name)] if name in left else rx1.at[right.index(name)]

    for f, rx0, rx1, _, _, s0, s1, y, p, m in reduces:
        def add(name, src, k, to, lo=0, hi=R, into=None, f=f, rx0=rx0, rx1=rx1):
            r.add(f + name, src.at[k, lo:hi], landing(into or name, rx0, rx1).at[lo:hi], to)
        add("c2", s1, 7, m)
        add("y6", s0, 7, y)
        add("c1", s1, 6, p)
        add("g2", s1, 4, p)
        add("y2", s0, 4, y)
        add("g1", s1, 3, m)
        add("y3", s0, 5, y)
        add("y0", s0, 1, y)
        add("ct", s0, 6, p, 0, H, "cc")
        add("cb", s0, 6, m, H, R, "cc")
        add("f2", s1, 5, m)
        add("f1", s1, 2, p)
        add("pmb", s0, 2, p, H, R, "pm")
        add("pmt", s0, 2, p, 0, H, "pm")
        add("ppt", s0, 3, m, 0, H, "pp")
        add("ppb", s0, 3, m, H, R, "pp")
        add("e1", s1, 1, y)

    def core_copy(k):
        return pltpu.make_async_remote_copy(
            src_ref=im.at[rows_at(k, 2 * R), 0:D], dst_ref=rx_core.at[k],
            send_sem=c_send.at[k], recv_sem=c_recv.at[k], device_id=core, device_id_type=MESH)

    def place_of(table, k):
        value = jnp.int32(4)
        for n, entry in enumerate(table):
            value = jnp.where(k == entry, jnp.int32(n), value)
        return value

    def put(k, value, k0, k1, s0, s1):
        value0, value1 = value[:, 0:S], value[:, S:2 * D]
        k0[place_of(KEEP0, k)] = value0
        k1[place_of(KEEP1, k)] = value1
        s0[k] = value0.astype(BF16)
        s1[k] = value1.astype(BF16)

    def send(k, f):
        for slot, names in ((7, ("c2", "y6")), (6, ("c1",)), (4, ("g2", "y2")), (3, ("g1",)), (5, ("y3",)), (1, ("y0",))):
            @pl.when(k == slot)
            def _(names=names):
                r.start(*[f + name for name in names])

    def event(family, do):
        for f, rx0, rx1, k0, k1, s0, s1, *_ in reduces:
            if f == family:
                do(f, lambda name: landing(name, rx0, rx1), k0, k1, s0, s1)

    def after(name, f, rx, k0, k1, s0, s1):
        def got(name, lo=0, hi=R):
            return rx(name)[lo:hi].astype(F32)
        if name == "y6":
            r.landed(f + "y6")
            s0[6] = (k0[KEEP0.index(6)] + got("y6")).astype(BF16)
            r.start(f + "ct", f + "cb")
        elif name == "c2":
            r.landed(f + "c2")
            s1[5] = (k1[KEEP1.index(5)] + got("c2")).astype(BF16)
            r.start(f + "f2")
        elif name == "c1":
            r.landed(f + "c1")
            s1[2] = (k1[KEEP1.index(2)] + got("c1")).astype(BF16)
            r.start(f + "f1")
        elif name == "y2":
            r.landed(f + "y2")
            s0[2, H:R] = (k0[KEEP0.index(2), H:R] + got("y2", H, R)).astype(BF16)
            r.start(f + "pmb")
        elif name == "ct":
            r.landed(f + "ct")
            s0[2, 0:H] = (k0[KEEP0.index(2), 0:H] + got("y2", 0, H) + got("cc", 0, H)).astype(BF16)
            r.start(f + "pmt")
        elif name == "y3":
            r.landed(f + "y3")
            s0[3, 0:H] = (k0[KEEP0.index(3), 0:H] + got("y3", 0, H)).astype(BF16)
            r.start(f + "ppt")
        elif name == "cb":
            r.landed(f + "cb")
            s0[3, H:R] = (k0[KEEP0.index(3), H:R] + got("y3", H, R) + got("cc", H, R)).astype(BF16)
            r.start(f + "ppb")
        elif name == "e1":
            r.landed(f + "g2", f + "f2")
            s1[1] = (k1[KEEP1.index(1)] + got("g2") + got("f2")).astype(BF16)
            r.start(f + "e1")

    def give(k):
        mine, theirs = (pl.ds(pl.multiple_of(k * 2 * R + half, R), R) for half in (0, R))
        part = jnp.dot(w[theirs, :], tx[...], preferred_element_type=F32)
        im[mine, 0:D] = part[:, 0:D].astype(BF16)
        im[theirs, 0:D] = part[:, D:2 * D].astype(BF16)
        core_copy(k).start()

    def follow(n, parity):
        for family, name, at in EVENTS:
            if at < 15 and at % 2 == parity:
                @pl.when(n == at // 2)
                def _(family=family, name=name):
                    event(family, functools.partial(after, name))

    def round_(n, _):
        k = pick(ORDER, n)
        part = lax.dot_general(w[:, rows_at(k, R)], im[:, D:3 * D], (((0,), (0,)), ((), ())), preferred_element_type=F32)
        put(k, part, keep_t0, keep_t1, st_t0, st_t1)
        send(k, "t")
        follow(n, 0)

        @pl.when(n < 7)
        def _():
            give(pick(ORDER, n + 1))

        core_copy(k).wait_recv()
        part = jnp.dot(w[pl.ds(pl.multiple_of(k * 2 * R, R), R), :], tx[...], preferred_element_type=F32)
        part = part + jnp.concatenate([rx_core[k, 0:R], rx_core[k, R:2 * R]], axis=1).astype(F32)
        put(k, part, keep_i0, keep_i1, st_i0, st_i1)
        send(k, "i")
        follow(n, 1)
        return 0

    give(ORDER[0])
    lax.fori_loop(0, 8, round_, 0)
    for family, name, at in EVENTS:
        if at == 15:
            event(family, functools.partial(after, name))

    times = jnp.exp(jnp.broadcast_to(log_temp[...], (1, S)))
    outs = {"i": (out_img_tan, out_img), "t": (out_txt_tan, out_txt)}

    def finish_left(f, rx, k0, k1, s0, s1):
        r.landed(f + "y0", f + "pmb", f + "pmt", f + "ppt", f + "ppb")
        total = k0[0] + rx("y0")[...].astype(F32) + rx("pm")[...].astype(F32) + rx("pp")[...].astype(F32)
        outs[f][0][:, 0:S] = times * total

    def finish_right(f, rx, k0, k1, s0, s1):
        r.landed(f + "f1", f + "g1", f + "e1")
        total = k1[0] + rx("f1")[...].astype(F32) + rx("g1")[...].astype(F32) + rx("e1")[...].astype(F32)
        total = jnp.broadcast_to(times[:, 0:1], total.shape) * total
        outs[f][0][:, S:D] = total[:, 0:D - S]
        outs[f][1][...] = total[:, D - S:]

    event("t", finish_left)
    event("i", finish_left)
    event("t", finish_right)
    event("i", finish_right)
    r.drain()
    for k in range(8):
        core_copy(k).wait_send()


def copier(a, b, c, d, e, f, g, h, sem):
    copies = [pltpu.make_async_copy(src, dst, sem.at[n])
              for n, (src, dst) in enumerate(((a, e), (b, f), (c, g), (d, h)))]
    for copy in copies:
        copy.start()
    for copy in copies:
        copy.wait()


def body(img_embed, img_tangent, txt_embed, txt_tangent, labels, log_temp, bias, cotangent):
    R, D = txt_embed.shape
    S = split(D)
    vmem = pl.BlockSpec(memory_space=pltpu.VMEM)
    anym = pl.BlockSpec(memory_space=pl.ANY)
    out = pltpu.VMEM((R, D), F32)
    dma = pltpu.SemaphoreType.DMA
    grads = pl.pallas_call(
        kernel,
        out_shape=[out] * 4,
        in_specs=[anym] * 8,
        out_specs=[vmem] * 4,
        scratch_shapes=[
            pltpu.VMEM((16 * R, 3 * D), BF16),
            pltpu.VMEM((8 * R, 2 * D), BF16),
            pltpu.VMEM((R, D), BF16),
            pltpu.VMEM((16 * R, 8 * R), BF16),
            pltpu.VMEM((16 * R, R), jnp.int32),
            pltpu.VMEM((8, 2 * R, D), BF16),
        ] + [pltpu.VMEM((7, R, S), BF16), pltpu.VMEM((7, R, 2 * D - S), BF16)] * 2
        + [pltpu.VMEM((5, R, S), F32), pltpu.VMEM((5, R, 2 * D - S), F32)] * 2
        + [pltpu.VMEM((8, R, S), BF16), pltpu.VMEM((8, R, 2 * D - S), BF16)] * 2
        + [pltpu.VMEM((1, 1), F32)] * 3 + [pltpu.VMEM((16, R), jnp.int32)]
        + [dma((8,)), dma((N_GATHER,)), dma((N_GATHER,)), dma((N_REDUCE,)), dma((N_REDUCE,)), dma((8,)), dma((8,))],
        compiler_params=pltpu.CompilerParams(
            collective_id=0, has_side_effects=True, vmem_limit_bytes=60 * 2 ** 20),
    )(log_temp.reshape(1, 1), bias.reshape(1, 1), cotangent.reshape(1, 1), labels.reshape(16, R), img_embed, img_tangent, txt_embed, txt_tangent)
    grads = pl.pallas_call(
        copier, out_shape=[jax.ShapeDtypeStruct((R, D), F32)] * 4, in_specs=[vmem] * 4, out_specs=[anym] * 4,
        scratch_shapes=[dma((4,))],
    )(*[pltpu.with_memory_space_constraint(grad, pltpu.VMEM) for grad in grads])
    grad_img, grad_img_tangent, grad_txt, grad_txt_tangent = grads
    return grad_img, grad_img_tangent, grad_txt, grad_txt_tangent


def solution(mesh):
    rows = P(("img", "txt"), None)
    cols = P(("txt", "img"), None)
    return jax.shard_map(
        body, mesh=mesh,
        in_specs=(rows, rows, cols, cols, P("img"), P(), P(), P()),
        out_specs=(rows, rows, cols, cols), check_vma=False)
```

profile of v0, /device:TPU:0, one launch (start us, length us, event | category | flops | bytes accessed | tf_op | source)
XLA Modules:
  0.0 90.0 jit_solution(1264584811732180678)
XLA Ops:
  2.6 86.0 %shard_map.111 = (f32[128,1152]{1,0:T(8,128)S(1)}, f32[128,1152]{1,0:T(8,128)S(1)}, f32[128,1152]{1,0:T(8,128)S(1)}, f32[128,1152]{1,0:T(8,128)S(1)}) custom-call(f32[1,1]{1,0:T(1,128)} %bitcast.4.log_temp_in, f32[1,1]{1,0:T(1,128)} %bitcast.5.bias_in, f32[1,1]{1,0:T(1,128)} %bitcast.6.cotangent_in, s32[16,128]{1,0:T(8,128)} %bitcast.7, ...), custom_call_target="tpu_custom_call" | custom-call | tf_op jit(solution)/shard_map/pallas_call | solution.py:415
  88.6 1.4 %shard_map.112 = (f32[128,1152]{1,0:T(8,128)}, f32[128,1152]{1,0:T(8,128)}, f32[128,1152]{1,0:T(8,128)}, f32[128,1152]{1,0:T(8,128)}) custom-call(f32[128,1152]{1,0:T(8,128)S(1)} %get-tuple-element.8.a, f32[128,1152]{1,0:T(8,128)S(1)} %get-tuple-element.9.b, f32[128,1152]{1,0:T(8,128)S(1)} %get-tuple-element.10.c, f32[128,1152]{1,0:T(8,128)S(1)} %get-tuple-element.11.d), custom_call_target="tpu_custom_call" | custom-call | tf_op jit(solution)/shard_map/pallas_call | solution.py:435
where the time goes:
time: 90.2 us; the launch traced here: 90 us
  Pallas kernels  87.4 us (97%)
  between operations  2.58 us (3%)
    pallas_call x1, Pallas kernels, body(): pl.pallas_call(kernel, out_shape=[out] * 4, in_specs=[anym] * 8, out_spec...  86 us

commit v1 on v0

--- a/solution.py
+++ b/solution.py
@@ -225,14 +225,19 @@
         arrive((6, 7))
 
     def part(s, _):
-        for at, do in ((0, first), (2, forward), (4, second), (6, second_img), (9, third)):
+        for at, do in ((0, first), (2, forward), (4, second)):
             @pl.when(s == at)
             def _(do=do):
                 do()
 
         return tile(s, 0)
 
-    lax.fori_loop(0, 12, part, 0)
+    lax.fori_loop(0, 6, part, 0)
+    second_img()
+    rows = pl.ds(8 * R, 4 * R)
+    weigh(lax.dot_general(im[rows, 0:2 * D], tx[0:6 * R, :], (((1,), (1,)), ((), ())), preferred_element_type=F32), rows, 0, 6)
+    third()
+    lax.fori_loop(9, 12, tile, 0)
     third_img()
     rows = pl.ds(12 * R, 4 * R)
     weigh(lax.dot_general(im[rows, 0:2 * D], tx[...], (((1,), (1,)), ((), ())), preferred_element_type=F32), rows, 0, 8)

time: 90.2 us -> 90.6 us (level)
  no operation moved by 1% of the time
where the time goes in v1:
time: 90.6 us; the launch traced here: 89.9 us
  Pallas kernels  87.3 us (96%)
  between operations  2.58 us (3%)
    pallas_call x1, Pallas kernels, body(): pl.pallas_call(kernel, out_shape=[out] * 4, in_specs=[anym] * 8, out_spec...  85.9 us

profile of v1, /device:TPU:0, one launch (start us, length us, event | category | flops | bytes accessed | tf_op | source)
XLA Modules:
  0.0 89.9 jit_solution(14650191003903760343)
XLA Ops:
  2.6 85.9 %shard_map.111 = (f32[128,1152]{1,0:T(8,128)S(1)}, f32[128,1152]{1,0:T(8,128)S(1)}, f32[128,1152]{1,0:T(8,128)S(1)}, f32[128,1152]{1,0:T(8,128)S(1)}) custom-call(f32[1,1]{1,0:T(1,128)} %bitcast.4.log_temp_in, f32[1,1]{1,0:T(1,128)} %bitcast.5.bias_in, f32[1,1]{1,0:T(1,128)} %bitcast.6.cotangent_in, s32[16,128]{1,0:T(8,128)} %bitcast.7, ...), custom_call_target="tpu_custom_call" | custom-call | tf_op jit(solution)/shard_map/pallas_call | solution.py:420
  88.4 1.4 %shard_map.112 = (f32[128,1152]{1,0:T(8,128)}, f32[128,1152]{1,0:T(8,128)}, f32[128,1152]{1,0:T(8,128)}, f32[128,1152]{1,0:T(8,128)}) custom-call(f32[128,1152]{1,0:T(8,128)S(1)} %get-tuple-element.8.a, f32[128,1152]{1,0:T(8,128)S(1)} %get-tuple-element.9.b, f32[128,1152]{1,0:T(8,128)S(1)} %get-tuple-element.10.c, f32[128,1152]{1,0:T(8,128)S(1)} %get-tuple-element.11.d), custom_call_target="tpu_custom_call" | custom-call | tf_op jit(solution)/shard_map/pallas_call | solution.py:440
